TPU v7x, 512 devices: a whole 4x8x8 slice. The times are simulated.
512 devices in a mesh: brow: 16 (over y, z_lo), bcol: 32 (over x, z_hi, core).
Axes of the slice: x: 4, y: 8, z: 8 (z_hi: 4, z_lo: 2; z = z_hi * 2 + z_lo), core: 2. Of those that a mesh axis runs over, the one named last changes fastest.
Arguments:
- scores: float32 [32, 1024, 128], P('bcol', 'brow'), may hold values from 0.01 to 32
- degree: int32 [32, 1024], P('bcol', 'brow'), may hold values from 50 to 200
- seed_mask: int32 [32, 1024], P('bcol', 'brow'), may hold values 0 or 1
- tiles: bfloat16 [16, 32, 64, 128, 128], P('brow', 'bcol'), may hold values from 0 to 2, as said below
- tile_list: int32 [16, 32, 2, 64], P('brow', 'bcol'), may hold values from 0 to 15, as said below
- tile_count: int32 [16, 32], P('brow', 'bcol'), may hold values from 1 to 64, as said below
Outputs:
- propagated: float32 [32, 1024, 128], P('bcol', 'brow')
Inputs may be any that keep to these rules, and one draw needn't show every extreme that they name: Slots 0 to tile_count - 1 of a device are live, the others empty; some device holds 64 live tiles. `tile_list`: entry 0 is below 16, entry 1 below 8; the live slots of a device name distinct tile blocks (a, b) with b >= a; every block (a, a) is named by a live slot. `tiles`: entries are nonnegative; a tile with a == b is symmetric and has a nonzero entry in every row; empty slots hold finite values.
All inputs are finite; a program needn't handle non-finite values. No bound on the sum of `seed_mask` on one device may be relied on, other than what follows from the above.
Results may differ from a plain program's by a relative error of at most 0.0007.
Values may be sent and summed in bfloat16 or wider, within the bound.
No kernel may reach another device: no remote copies, remote signals or barrier semaphores. Data moves between devices by JAX's collectives and lax.ppermute only.
A program may use at most 64 MiB of HBM per device.

v0:
```python
import math
import jax
import jax.numpy as jnp
from jax import lax
from jax.sharding import PartitionSpec as P

SWEEPS = 2


def spread(value, axis, source):
    kept = jnp.where(lax.axis_index(axis) == source, value, 0).astype(value.dtype)
    return lax.psum(kept, axis)


def row_weights(field):
    total = jnp.sum(field, axis=-1, keepdims=True)
    share = field / total
    entropy = -jnp.sum(share * jnp.log(share), axis=-1, keepdims=True)
    return (2.0 - entropy / math.log(field.shape[-1])) * field


def column_scatter(col_flat):
    return lax.psum_scatter(col_flat, "brow", scatter_dimension=0, tiled=True)


def on_device(scores, degree, seed_mask, tiles, tile_list, tile_count):
    n_brow = lax.axis_size("brow")
    n_bcol = lax.axis_size("bcol")
    ratio = n_bcol // n_brow
    rows_dev = scores.shape[1]
    classes = scores.shape[2]
    capacity = tiles.shape[2]
    tile_size = tiles.shape[-1]
    col_tiles = n_brow * rows_dev // tile_size
    row_tiles = ratio * col_tiles
    my_row = lax.axis_index("brow")
    my_col = lax.axis_index("bcol")
    stored = tiles[0, 0].astype(jnp.float32)
    local_row = tile_list[0, 0, 0]
    local_col = tile_list[0, 0, 1]
    live = jnp.arange(capacity, dtype=jnp.int32) < tile_count[0, 0]
    same = my_row + n_brow * local_row == my_col + n_bcol * local_col
    row_onehot = (
        (local_row[:, None] == jnp.arange(row_tiles, dtype=jnp.int32)[None, :]) & live[:, None]
    ).astype(jnp.float32)
    col_onehot = (
        (local_col[:, None] == jnp.arange(col_tiles, dtype=jnp.int32)[None, :])
        & (live & jnp.logical_not(same))[:, None]
    ).astype(jnp.float32)
    initial = scores[0]
    seeded = seed_mask[0][:, None] > 0
    scale = degree[0].astype(jnp.float32)[:, None]
    field = initial
    for sweep in range(SWEEPS):
        message = row_weights(field)
        col_range = lax.all_gather(message, "brow", axis=0, tiled=True)
        col_blocks = col_range.reshape(col_tiles, tile_size, classes)
        pieces = []
        for half in range(ratio):
            got = spread(col_range, "bcol", my_row + n_brow * half)
            pieces.append(got.reshape(col_tiles, tile_size, classes))
        row_blocks = jnp.stack(pieces, axis=1).reshape(row_tiles, tile_size, classes)
        col_pick = col_blocks[local_col]
        row_pick = row_blocks[local_row]
        forward = jnp.einsum("sij,sjk->sik", stored, col_pick, precision=lax.Precision.HIGHEST)
        mirror = jnp.einsum("sji,sjk->sik", stored, row_pick, precision=lax.Precision.HIGHEST)
        row_part = jnp.einsum("sl,sik->lik", row_onehot, forward, precision=lax.Precision.HIGHEST)
        col_part = jnp.einsum("sl,sik->lik", col_onehot, mirror, precision=lax.Precision.HIGHEST)
        row_part = (
            row_part.reshape(col_tiles, ratio, tile_size, classes)
            .transpose(1, 0, 2, 3)
            .reshape(ratio, n_brow * rows_dev, classes)
        )
        col_flat = col_part.reshape(n_brow * rows_dev, classes)
        moved = lax.all_to_all(row_part, "brow", split_axis=1, concat_axis=1, tiled=True)
        col_total = column_scatter(col_flat)
        arranged = moved.reshape(ratio * n_brow, rows_dev, classes)
        row_total = lax.psum_scatter(arranged, "bcol", scatter_dimension=0, tiled=True)[0]
        total = row_total + col_total
        field = jnp.where(seeded, initial, total / scale)
    return field[None]


def solution(mesh):
    placed = (
        P("bcol", "brow", None),
        P("bcol", "brow"),
        P("bcol", "brow"),
        P("brow", "bcol", None, None, None),
        P("brow", "bcol", None, None),
        P("brow", "bcol"),
    )
    return jax.shard_map(
        on_device, mesh=mesh, in_specs=placed, out_specs=P("bcol", "brow", None), check_vma=False
    )
```

profile of v0, /device:TPU:8, one launch (start us, length us, event | category | flops | bytes accessed | tf_op | source)
XLA Modules:
  0.0 1069.0 jit_solution(9725051248601173599)
XLA Ops:
  9.4 35.8 %all_gather.6 = f32[1024,128]{1,0:T(8,128)S(1)} all-gather(f32[64,128]{1,0:T(8,128)S(1)} %bitcast_multiply_fusion), channel_id=1, replica_groups=mesh['brow'=16,'bcol'=32] {'brow'}, dimensions={0}, use_global_device_ids=true | all-gather | bytes 557056 | tf_op jit(solution)/shard_map/all_gather | solution.py:56
  47.1 2.8 gather_fusion
  49.9 7.6 convolution_bitcast_fusion.3
  58.1 5.4 copy.30
  63.6 3.7 fusion.15
  69.4 6.9 all-to-all-start
  76.5 268.0 %all-reduce.7.cloned.1.call-done = (f32[8,1,128,128]{3,2,1,0:T(8,128)}, f32[8,1,128,128]{3,2,1,0:T(8,128)}) async-done(((f32[8,1,128,128]{3,2,1,0:T(8,128)}, f32[8,1,128,128]{3,2,1,0:T(8,128)}), (f32[8,1,128,128]{3,2,1,0:T(8,128)}, f32[8,1,128,128]{3,2,1,0:T(8,128)})) %all-reduce.7.cloned.1.call-update) | async-done | bytes 1048592 | tf_op jit(solution)/shard_map/psum | solution.py:12
  348.5 7.6 convolution_bitcast_fusion.2
  356.1 5.4 copy.35
  361.5 3.7 fusion.25
  368.5 67.4 %reduce-scatter.7.cloned.1.call-done = f32[64,128]{1,0:T(8,128)} async-done(((f32[1024,128]{1,0:T(8,128)}), f32[64,128]{1,0:T(8,128)}) %reduce-scatter.7.cloned.1.call-update) | async-done | bytes 32784 | tf_op jit(solution)/shard_map/reduce_scatter | solution.py:23
  435.9 102.8 %reduce-scatter.5.cloned.1.call-done = f32[1,64,128]{2,1,0:T(8,128)} async-done(((f32[32,64,128]{2,1,0:T(8,128)}), f32[1,64,128]{2,1,0:T(8,128)}) %reduce-scatter.5.cloned.1.call-update) | async-done | bytes 32784 | tf_op jit(solution)/shard_map/reduce_scatter | solution.py:78
  540.0 33.6 %all_gather.7 = f32[1024,128]{1,0:T(8,128)S(1)} all-gather(f32[64,128]{1,0:T(8,128)S(1)} %broadcast_multiply_fusion), channel_id=1, replica_groups=mesh['brow'=16,'bcol'=32] {'brow'}, dimensions={0}, use_global_device_ids=true | all-gather | bytes 557056 | tf_op jit(solution)/shard_map/all_gather | solution.py:56
  574.7 2.8 gather_fusion.2
  577.5 7.6 convolution_bitcast_fusion.1
  585.1 5.4 copy.38
  590.5 3.7 fusion.13
  596.3 7.9 all-to-all-start.1
  604.5 261.4 %all-reduce.5.cloned.1.call-done = (f32[8,1,128,128]{3,2,1,0:T(8,128)}, f32[8,1,128,128]{3,2,1,0:T(8,128)}) async-done(((f32[8,1,128,128]{3,2,1,0:T(8,128)}, f32[8,1,128,128]{3,2,1,0:T(8,128)}), (f32[8,1,128,128]{3,2,1,0:T(8,128)}, f32[8,1,128,128]{3,2,1,0:T(8,128)})) %all-reduce.5.cloned.1.call-update) | async-done | bytes 1048592 | tf_op jit(solution)/shard_map/psum | solution.py:12
  870.0 7.6 convolution_bitcast_fusion
  877.6 5.4 copy.45
  883.0 3.7 fusion.23
  889.9 67.6 %reduce-scatter.11.cloned.1.call-done = f32[64,128]{1,0:T(8,128)} async-done(((f32[1024,128]{1,0:T(8,128)}), f32[64,128]{1,0:T(8,128)}) %reduce-scatter.11.cloned.1.call-update) | async-done | bytes 32784 | tf_op jit(solution)/shard_map/reduce_scatter | solution.py:23
  957.5 103.1 %reduce-scatter.9.cloned.1.call-done = f32[1,64,128]{2,1,0:T(8,128)} async-done(((f32[32,64,128]{2,1,0:T(8,128)}), f32[1,64,128]{2,1,0:T(8,128)}) %reduce-scatter.9.cloned.1.call-update) | async-done | bytes 32784 | tf_op jit(solution)/shard_map/reduce_scatter | solution.py:78
  (54 shorter events, 27.9 us)
Async XLA Ops:
  6.5 43.3 %copy-start = (bf16[1,1,64,128,128]{4,3,2,1,0:T(8,128)(2,1)S(1)}, bf16[1,1,64,128,128]{4,3,2,1,0:T(8,128)(2,1)}, u32[]{:S(2)}) copy-start(bf16[1,1,64,128,128]{4,3,2,1,0:T(8,128)(2,1)} %param.9) | copy-start | bytes 6291460
  6.5 337.9 %all-reduce.7.cloned.1.call-start = ((), (), s32[]{:S(2)}) async-start(), calls=%async_computation.11 | async-start | bytes 2097152 | tf_op jit(solution)/shard_map/psum | solution.py:12
  58.1 5.4 copy-start.2
  69.4 296.8 %all-to-all-start = ((f32[2,1024,128]{2,0,1:T(2,128)}), f32[2,1024,128]{2,0,1:T(2,128)}, u32[]{:S(2)}, u32[]{:S(2)}) async-start(f32[2,1024,128]{2,0,1:T(2,128)} %copy.32), calls=%async_computation | async-start | bytes 2097152 | tf_op jit(solution)/shard_map/all_to_all | solution.py:75
  76.2 359.7 %reduce-scatter.7.cloned.1.call-start = ((), (), s32[]{:S(2)}) async-start(), calls=%async_computation.7 | async-start | bytes 557056 | tf_op jit(solution)/shard_map/reduce_scatter | solution.py:23
  361.5 7.0 copy-start.3
  361.5 7.0 copy-start.4
  361.5 177.3 %copy-start.1 = (f32[1,64,128]{2,1,0:T(8,128)S(1)}, f32[1,64,128]{2,1,0:T(8,128)}, u32[]{:S(2)}) copy-start(f32[1,64,128]{2,1,0:T(8,128)} %param.6) | copy-start | bytes 98308
  366.1 172.7 %reduce-scatter.5.cloned.1.call-start = ((), (), s32[]{:S(2)}) async-start(), calls=%async_computation.6 | async-start | bytes 1081344 | tf_op jit(solution)/shard_map/reduce_scatter | solution.py:78
  368.5 497.5 %all-reduce.5.cloned.1.call-start = ((), (), s32[]{:S(2)}) async-start(), calls=%async_computation.10 | async-start | bytes 2097152 | tf_op jit(solution)/shard_map/psum | solution.py:12
  596.3 291.4 %all-to-all-start.1 = ((f32[2,1024,128]{2,0,1:T(2,128)}), f32[2,1024,128]{2,0,1:T(2,128)}, u32[]{:S(2)}, u32[]{:S(2)}) async-start(f32[2,1024,128]{2,0,1:T(2,128)} %copy.40), calls=%async_computation.3 | async-start | bytes 2097152 | tf_op jit(solution)/shard_map/all_to_all | solution.py:75
  604.2 353.3 %reduce-scatter.11.cloned.1.call-start = ((), (), s32[]{:S(2)}) async-start(), calls=%async_computation.9 | async-start | bytes 557056 | tf_op jit(solution)/shard_map/reduce_scatter | solution.py:23
  887.6 173.1 %reduce-scatter.9.cloned.1.call-start = ((), (), s32[]{:S(2)}) async-start(), calls=%async_computation.8 | async-start | bytes 1081344 | tf_op jit(solution)/shard_map/reduce_scatter | solution.py:78
Sparse Core Ops, SparseCore 0:
  46.4 297.9 all-reduce.6
  366.2 69.6 reduce-scatter.6
  440.3 98.4 reduce-scatter.4
  574.8 291.1 all-reduce.4
  887.7 69.7 reduce-scatter.10
  962.4 98.2 reduce-scatter.8
where the time goes:
time: 1070 us
  waiting for transfers between devices  870 us (81%)
  blocking collectives  69.4 us (6%)
  matrix products  45 us (4%)
  local copies, waits for them, and re-layouts  43.4 us (4%)
  starting transfers between devices  15.4 us (1%)
  between operations  14.3 us (1%)
  other arithmetic  11 us (1%)
    psum x2, waiting for transfers between devices, spread(): return lax.psum(kept, axis)  529 us
    reduce_scatter x2, waiting for transfers between devices, on_device(): lax.psum_scatter(arranged, 'bcol', scatter_dimension=0, tiled=True)[0]  206 us
    reduce_scatter x2, waiting for transfers between devices, column_scatter(): return lax.psum_scatter(col_flat, 'brow', scatter_dimension=0, tiled=True)  135 us
    all_gather x2, blocking collectives, on_device(): col_range = lax.all_gather(message, 'brow', axis=0, tiled=True)  69.4 us
  transfers between devices with their start and end apart: 8, of which 6 were waited for; matrix products, arithmetic and copies ran while one was open for 9% of the time, Pallas kernels for 0%

commit v1 on v0

--- a/solution.py
+++ b/solution.py
@@ -9,7 +9,7 @@
 
 def spread(value, axis, source):
     kept = jnp.where(lax.axis_index(axis) == source, value, 0).astype(value.dtype)
-    return lax.psum(kept, axis)
+    return jnp.sum(lax.all_gather(kept, axis), axis=0)
 
 
 def row_weights(field):

time: 1070 us -> 964 us (0.901)
  the two profiles are of different devices: /device:TPU:8 before, /device:TPU:2 now
where the time goes in v1:
time: 964 us; the launch traced here: 963 us
  waiting for transfers between devices  702 us (73%)
  blocking collectives  121 us (13%)
  matrix products  45.4 us (5%)
  other arithmetic  40.4 us (4%)
  local copies, waits for them, and re-layouts  39.1 us (4%)
  between operations  14.3 us (1%)
    all_gather x4, waiting for transfers between devices, spread(): return jnp.sum(lax.all_gather(kept, axis), axis=0)  413 us
    reduce_scatter x2, waiting for transfers between devices, column_scatter(): return lax.psum_scatter(col_flat, 'brow', scatter_dimension=0, tiled=True)  147 us
    reduce_scatter x2, waiting for transfers between devices, on_device(): lax.psum_scatter(arranged, 'bcol', scatter_dimension=0, tiled=True)[0]  140 us
    all_gather x2, blocking collectives, on_device(): col_range = lax.all_gather(message, 'brow', axis=0, tiled=True)  70.8 us
    all_to_all x2, blocking collectives, on_device(): lax.all_to_all(row_part, 'brow', split_axis=1, concat_axis=1, tiled=True)  50.2 us
    reduce_sum x4, other arithmetic, spread(): return jnp.sum(lax.all_gather(kept, axis), axis=0)  29.4 us
  transfers between devices with their start and end apart: 8, of which 8 were waited for; matrix products, arithmetic and copies ran while one was open for 12% of the time, Pallas kernels for 0%

profile of v1, /device:TPU:2, one launch (start us, length us, event | category | flops | bytes accessed | tf_op | source)
XLA Modules:
  0.0 963.3 jit_solution(1601190413146909781)
XLA Ops:
  9.4 38.0 %all_gather.30 = f32[1024,128]{1,0:T(8,128)S(1)} all-gather(f32[64,128]{1,0:T(8,128)S(1)} %bitcast_multiply_fusion), channel_id=1, replica_groups=mesh['brow'=16,'bcol'=32] {'brow'}, dimensions={0}, use_global_device_ids=true | all-gather | bytes 557056 | tf_op jit(solution)/shard_map/all_gather | solution.py:56
  53.5 7.7 convolution_bitcast_fusion.3
  61.2 5.5 copy.26
  71.5 25.0 %all_to_all.10 = f32[2,1024,128]{2,0,1:T(2,128)S(1)} all-to-all(f32[2,1024,128]{2,0,1:T(2,128)S(1)} %copy.28), channel_id=1, replica_groups=mesh['brow'=16,'bcol'=32] {'brow'}, dimensions={1} | all-to-all | bytes 2097152 | tf_op jit(solution)/shard_map/all_to_all | solution.py:75
  97.9 87.2 %all-gather.9.cloned.1.call-done = f32[32768,128]{1,0:T(8,128)} async-done(((f32[1024,128]{1,0:T(8,128)}), f32[32768,128]{1,0:T(8,128)}) %all-gather.9.cloned.1.call-update) | async-done | bytes 16777232 | tf_op jit(solution)/shard_map/all_gather | solution.py:12
  185.1 7.4 reduce_sum.74
  192.5 118.7 %all-gather.11.cloned.1.call-done = f32[32768,128]{1,0:T(8,128)} async-done(((f32[1024,128]{1,0:T(8,128)}), f32[32768,128]{1,0:T(8,128)}) %all-gather.11.cloned.1.call-update) | async-done | bytes 16777232 | tf_op jit(solution)/shard_map/all_gather | solution.py:12
  311.2 7.4 reduce_sum.75
  322.6 7.5 convolution_bitcast_fusion.2
  330.2 5.4 copy.31
  340.4 70.0 %reduce-scatter.5.cloned.1.call-done = f32[1,64,128]{2,1,0:T(8,128)} async-done(((f32[32,64,128]{2,1,0:T(8,128)}), f32[1,64,128]{2,1,0:T(8,128)}) %reduce-scatter.5.cloned.1.call-update) | async-done | bytes 32784 | tf_op jit(solution)/shard_map/reduce_scatter | solution.py:78
  410.4 73.7 %reduce-scatter.7.cloned.1.call-done = f32[64,128]{1,0:T(8,128)} async-done(((f32[1024,128]{1,0:T(8,128)}), f32[64,128]{1,0:T(8,128)}) %reduce-scatter.7.cloned.1.call-update) | async-done | bytes 32784 | tf_op jit(solution)/shard_map/reduce_scatter | solution.py:23
  485.3 32.7 %all_gather.35 = f32[1024,128]{1,0:T(8,128)S(1)} all-gather(f32[64,128]{1,0:T(8,128)S(1)} %broadcast_multiply_fusion), channel_id=1, replica_groups=mesh['brow'=16,'bcol'=32] {'brow'}, dimensions={0}, use_global_device_ids=true | all-gather | bytes 557056 | tf_op jit(solution)/shard_map/all_gather | solution.py:56
  522.8 7.7 convolution_bitcast_fusion.1
  530.5 5.4 copy.34
  540.9 25.1 %all_to_all.11 = f32[2,1024,128]{2,0,1:T(2,128)S(1)} all-to-all(f32[2,1024,128]{2,0,1:T(2,128)S(1)} %copy.36), channel_id=1, replica_groups=mesh['brow'=16,'bcol'=32] {'brow'}, dimensions={1} | all-to-all | bytes 2097152 | tf_op jit(solution)/shard_map/all_to_all | solution.py:75
  567.5 88.7 %all-gather.13.cloned.1.call-done = f32[32768,128]{1,0:T(8,128)} async-done(((f32[1024,128]{1,0:T(8,128)}), f32[32768,128]{1,0:T(8,128)}) %all-gather.13.cloned.1.call-update) | async-done | bytes 16777232 | tf_op jit(solution)/shard_map/all_gather | solution.py:12
  656.1 7.4 reduce_sum.78
  663.5 118.5 %all-gather.15.cloned.1.call-done = f32[32768,128]{1,0:T(8,128)} async-done(((f32[1024,128]{1,0:T(8,128)}), f32[32768,128]{1,0:T(8,128)}) %all-gather.15.cloned.1.call-update) | async-done | bytes 16777232 | tf_op jit(solution)/shard_map/all_gather | solution.py:12
  782.0 7.4 reduce_sum.79
  793.5 7.5 convolution_bitcast_fusion
  801.0 5.4 copy.39
  811.1 70.2 %reduce-scatter.9.cloned.1.call-done = f32[1,64,128]{2,1,0:T(8,128)} async-done(((f32[32,64,128]{2,1,0:T(8,128)}), f32[1,64,128]{2,1,0:T(8,128)}) %reduce-scatter.9.cloned.1.call-update) | async-done | bytes 32784 | tf_op jit(solution)/shard_map/reduce_scatter | solution.py:78
  881.2 73.8 %reduce-scatter.11.cloned.1.call-done = f32[64,128]{1,0:T(8,128)} async-done(((f32[1024,128]{1,0:T(8,128)}), f32[64,128]{1,0:T(8,128)}) %reduce-scatter.11.cloned.1.call-update) | async-done | bytes 32784 | tf_op jit(solution)/shard_map/reduce_scatter | solution.py:23
  (62 shorter events, 45.5 us)
Async XLA Ops:
  6.5 46.9 %copy-start = (bf16[1,1,64,128,128]{4,3,2,1,0:T(8,128)(2,1)S(1)}, bf16[1,1,64,128,128]{4,3,2,1,0:T(8,128)(2,1)}, u32[]{:S(2)}) copy-start(bf16[1,1,64,128,128]{4,3,2,1,0:T(8,128)(2,1)} %param.9) | copy-start | bytes 6291460
  6.5 178.6 %all-gather.9.cloned.1.call-start = ((), (), s32[]{:S(2)}) async-start(), calls=%async_computation.10 | async-start | bytes 17301504 | tf_op jit(solution)/shard_map/all_gather | solution.py:12
  48.5 262.7 %all-gather.11.cloned.1.call-start = ((), (), s32[]{:S(2)}) async-start(), calls=%async_computation.11 | async-start | bytes 17301504 | tf_op jit(solution)/shard_map/all_gather | solution.py:12
  49.2 361.1 %reduce-scatter.5.cloned.1.call-start = ((), (), s32[]{:S(2)}) async-start(), calls=%async_computation.6 | async-start | bytes 1081344 | tf_op jit(solution)/shard_map/reduce_scatter | solution.py:78
  61.2 5.5 copy-start.2
  97.7 386.4 %reduce-scatter.7.cloned.1.call-start = ((), (), s32[]{:S(2)}) async-start(), calls=%async_computation.7 | async-start | bytes 557056 | tf_op jit(solution)/shard_map/reduce_scatter | solution.py:23
  335.6 4.7 copy-start.3
  335.6 4.7 copy-start.4
  335.6 148.5 %copy-start.1 = (f32[1,64,128]{2,1,0:T(8,128)S(1)}, f32[1,64,128]{2,1,0:T(8,128)}, u32[]{:S(2)}) copy-start(f32[1,64,128]{2,1,0:T(8,128)} %param.6) | copy-start | bytes 98308
  340.3 315.9 %all-gather.13.cloned.1.call-start = ((), (), s32[]{:S(2)}) async-start(), calls=%async_computation.12 | async-start | bytes 17301504 | tf_op jit(solution)/shard_map/all_gather | solution.py:12
  519.2 262.9 %all-gather.15.cloned.1.call-start = ((), (), s32[]{:S(2)}) async-start(), calls=%async_computation.13 | async-start | bytes 17301504 | tf_op jit(solution)/shard_map/all_gather | solution.py:12
  519.8 361.4 %reduce-scatter.9.cloned.1.call-start = ((), (), s32[]{:S(2)}) async-start(), calls=%async_computation.8 | async-start | bytes 1081344 | tf_op jit(solution)/shard_map/reduce_scatter | solution.py:78
  567.1 387.8 %reduce-scatter.11.cloned.1.call-start = ((), (), s32[]{:S(2)}) async-start(), calls=%async_computation.9 | async-start | bytes 557056 | tf_op jit(solution)/shard_map/reduce_scatter | solution.py:23
Sparse Core Ops, SparseCore 0:
  48.6 136.4 all-gather.8
  188.3 122.8 all-gather.10
  315.6 94.7 reduce-scatter.4
  413.3 70.7 reduce-scatter.6
  519.3 136.7 all-gather.12
  659.1 122.8 all-gather.14
  786.4 94.7 reduce-scatter.8
  884.2 70.6 reduce-scatter.10
